TPU v7x, 32 devices: a whole 2x2x4 slice. The times are simulated.
32 devices in a mesh: groups: 2 (over y), ctx: 4 (over z), head: 2 (over x), sub: 2 (over core).
Axes of the slice: x: 2, y: 2, z: 4, core: 2. Of those that a mesh axis runs over, the one named last changes fastest.
Arguments:
- queries: bfloat16 [1024, 4096], P(('groups', 'ctx'), ('head', 'sub')), parts along dimension 0, may hold values from -40 to 40
- keys_values: bfloat16 [1024, 8, 128], P(('groups', 'ctx'), 'head'), parts along dimension 0, may hold values from -5 to 5
- sinks: float32 [64], P(('head', 'sub')), may hold values from 0 to 4
- out_weight: bfloat16 [4096, 2880], P(('head', 'sub')), may hold values from -0.09375 to 0.09375
- residual_in: bfloat16 [1024, 2880], P(('groups', 'ctx'), ('head', 'sub')), parts along dimension 0, may hold values from -96 to 96
- norm_gain: float32 [2880], replicated, may hold values from 0.5 to 1.5
- expert_ids: int32 [1024, 4], P(('groups', 'ctx')), parts along dimension 0, may hold values from 0 to 15, all different within a row; in each aligned block of 128 rows (0 to 127, 128 to 255, ...) at most 40 rows name the same one
- gate_weights: float32 [1024, 4], P(('groups', 'ctx')), parts along dimension 0, may hold values from 0.05 to 1
- gate_up: bfloat16 [16, 2880, 2, 2880], P('ctx', None, None, ('head', 'sub')), may hold values from -0.109375 to 0.109375
- down_weight: bfloat16 [16, 2880, 2880], P('ctx', None, ('head', 'sub')), may hold values from -0.109375 to 0.109375
Outputs:
- block_out: bfloat16 [1024, 2880], P(('groups', 'ctx'), ('head', 'sub')), parts along dimension 0
There are 2 independent parts, one for each index of `groups`. A program takes and returns all parts, laid end to end along the dimension named above; an argument that names none is the same for every part. Nothing has to cross between parts.
Inputs may be any that keep to these rules, and one draw needn't show every extreme that they name: `expert_ids`: each row names 4 different experts; among the 128 rows of one index of ctx no expert is named by more than 40 rows, a bound that some block reaches.
All inputs are finite; a program needn't handle non-finite values.
Results may differ from a plain program's by a relative error of at most 0.015.
Values may be sent and summed in bfloat16 or wider, within the bound.
A program may use at most 192 MiB of HBM per device.

v0:
```python
import jax
import jax.numpy as jnp
from jax import lax
from jax.sharding import PartitionSpec as P

D = 2880
HEADS = 64
KV_HEADS = 8
HD = 64
WIN = 128
EXPERTS = 16
TOP = 4
CAP = 40


def from_behind(value, axis, steps):
    count = lax.axis_size(axis)
    leading, last = (max(0, -steps), min(count, count - steps))
    return lax.ppermute(value, axis, [(source, source + steps) for source in range(leading, last)])


def shards(
    queries,
    keys_values,
    sinks,
    out_weight,
    residual_in,
    norm_gain,
    expert_ids,
    gate_weights,
    gate_up,
    down_weight,
):
    tok_rows = queries.shape[0]
    local_heads = sinks.shape[0]
    group_size = HEADS // KV_HEADS
    edge_rows = from_behind(keys_values, "ctx", 1)
    window_kv = jnp.concatenate([edge_rows, keys_values], 0)
    shared_head = (lax.axis_index("sub") * local_heads + jnp.arange(local_heads)) // group_size
    key_heads = jnp.take(window_kv[..., :HD], shared_head, axis=1)
    value_heads = jnp.take(window_kv[..., HD:], shared_head, axis=1)
    query_heads = queries.reshape(tok_rows, local_heads, HD)
    scores = jnp.einsum(
        "qhd,khd->hqk", query_heads, key_heads, preferred_element_type=jnp.float32
    ) * HD ** (-0.5)
    offset = lax.axis_index("ctx") * tok_rows
    query_pos = offset + jnp.arange(tok_rows)
    key_pos = offset - WIN + jnp.arange(WIN + tok_rows)
    distance = query_pos[:, None] - key_pos[None, :]
    allowed = (distance >= 0) & (distance < WIN) & (key_pos[None, :] >= 0)
    masked = jnp.where(allowed[None], scores, -1e30)
    highest = jnp.maximum(masked.max(-1), sinks[:, None])
    weights = jnp.where(allowed[None], jnp.exp(scores - highest[..., None]), 0.0)
    totals = weights.sum(-1) + jnp.exp(sinks[:, None] - highest)
    weighed = jnp.einsum(
        "hqk,khd->qhd",
        weights.astype(jnp.bfloat16),
        value_heads,
        preferred_element_type=jnp.float32,
    )
    attended = (
        (weighed / totals.T[..., None]).astype(jnp.bfloat16).reshape(tok_rows, local_heads * HD)
    )
    width_share = residual_in.shape[1]
    column_start = lax.axis_index(("head", "sub")) * width_share
    projected_attn = jnp.dot(attended, out_weight, preferred_element_type=jnp.float32)
    own_columns = lax.dynamic_slice_in_dim(
        projected_attn, column_start, width_share, 1
    ) + residual_in.astype(jnp.float32)
    projected_attn = lax.dynamic_update_slice_in_dim(projected_attn, own_columns, column_start, 1)
    hidden_state = lax.psum(projected_attn.astype(jnp.bfloat16), ("head", "sub")).astype(
        jnp.float32
    )
    normed = (
        hidden_state
        * lax.rsqrt(jnp.mean(hidden_state * hidden_state, -1, keepdims=True) + 1e-05)
        * norm_gain
    ).astype(jnp.bfloat16)
    flat_ids = expert_ids.reshape(-1)
    one_hot = (flat_ids[:, None] == jnp.arange(EXPERTS)[None, :]).astype(jnp.int32)
    slot_rank = jnp.sum((jnp.cumsum(one_hot, 0) - one_hot) * one_hot, -1)
    slot_index = flat_ids * CAP + slot_rank
    slot_match = jnp.arange(EXPERTS * CAP)[:, None] == slot_index[None, :]
    picker = jnp.any(slot_match.reshape(EXPERTS * CAP, tok_rows, TOP), -1).astype(jnp.bfloat16)
    outgoing = jnp.dot(picker, normed, preferred_element_type=jnp.bfloat16).reshape(
        EXPERTS, 1, CAP, D
    )
    arrived = lax.all_to_all(outgoing, "ctx", split_axis=0, concat_axis=1, tiled=True)
    local_experts = gate_up.shape[0]
    share = gate_up.shape[3]
    expert_rows = arrived.reshape(local_experts, -1, D)
    projected = jnp.einsum(
        "erd,edf->erf",
        expert_rows,
        gate_up.reshape(local_experts, D, 2 * share),
        preferred_element_type=jnp.float32,
    )
    gate_part = projected[..., :share]
    up_part = projected[..., share:]
    activated = ((up_part + 1.0) * gate_part * jax.nn.sigmoid(1.702 * gate_part)).astype(
        jnp.bfloat16
    )
    resid_cols = lax.dynamic_slice_in_dim(hidden_state, column_start, width_share, 1)
    summed = lax.psum_scatter(
        jnp.einsum(
            "ecf,erf->cer", down_weight, activated, preferred_element_type=jnp.float32
        ).astype(jnp.bfloat16),
        ("head", "sub"),
        scatter_dimension=0,
        tiled=True,
    ).astype(jnp.float32)
    regrouped = summed.reshape(width_share, local_experts, -1, CAP)
    returned = lax.all_to_all(
        regrouped.astype(jnp.bfloat16), "ctx", split_axis=2, concat_axis=1, tiled=True
    ).astype(regrouped.dtype)
    combiner = jnp.sum(
        jnp.where(slot_match, gate_weights.reshape(-1)[None, :], 0.0).reshape(
            EXPERTS * CAP, tok_rows, TOP
        ),
        -1,
    )
    mixture = jnp.dot(
        returned.reshape(width_share, EXPERTS * CAP),
        combiner,
        precision=lax.Precision.HIGHEST,
        preferred_element_type=jnp.float32,
    ).T
    return (resid_cols + mixture).astype(jnp.bfloat16)


def solution(mesh):
    return jax.shard_map(
        shards,
        mesh=mesh,
        in_specs=(
            P(("groups", "ctx"), ("head", "sub")),
            P(("groups", "ctx"), "head", None),
            P(("head", "sub")),
            P(("head", "sub"), None),
            P(("groups", "ctx"), ("head", "sub")),
            P(),
            P(("groups", "ctx"), None),
            P(("groups", "ctx"), None),
            P("ctx", None, None, ("head", "sub")),
            P("ctx", None, ("head", "sub")),
        ),
        out_specs=P(("groups", "ctx"), ("head", "sub")),
        check_vma=False,
    )
```

profile of v0, /device:TPU:0, one launch (start us, length us, event | category | flops | bytes accessed | tf_op | source)
XLA Modules:
  0.0 270.8 jit_solution(8424025903728361341)
XLA Ops:
  6.5 1.0 copy.56
  7.6 4.9 %collective-permute-start = (bf16[128,4,128]{0,2,1:T(8,128)(2,1)S(1)}, bf16[128,4,128]{0,2,1:T(8,128)(2,1)S(1)}, u32[]{:S(2)}, u32[]{:S(2)}) collective-permute-start(bf16[128,4,128]{0,2,1:T(8,128)(2,1)S(1)} %copy.56), channel_id=1, source_target_pairs={{0,4},{4,8},{8,12},{1,5},{5,9},{9,13},{2,6},{6,10},{10,14},{3,7},{... | collective-permute-start | bytes 393224 | tf_op jit(solution)/shard_map/ppermute | solution.py:19
  12.6 0.8 copy.60
  13.4 0.1 eq.45
  13.5 1.2 reduce-window.6
  14.7 0.2 slice_reduce_fusion
  14.9 0.1 fusion.36
  15.1 1.1 copy.58
  16.4 0.6 gather_fusion.1
  17.0 0.6 fusion
  17.7 0.4 fusion.6
  18.2 0.6 gather_fusion
  18.8 0.5 fusion.10
  19.4 4.5 %fusion.48 = f32[128,2880]{0,1:T(8,128)S(1)} fusion(bf16[1024,2880]{0,1:T(8,128)(2,1)} %param.15, bf16[128,1024]{0,1:T(8,128)(2,1)S(1)} %bitcast.92), kind=kOutput, calls=%fused_computation.83 | convolution fusion | flops 754974720 | bytes 7634944 | tf_op jit(solution)/shard_map/dot_general | solution.py:66
  23.9 0.9 convert_element_type.47
  25.1 0.1 reduce_sum.40
  25.2 0.2 fusion.8
  25.4 34.9 %all-reduce.2.cloned.1.call-done = bf16[128,2880]{0,1:T(8,128)(2,1)} async-done(((bf16[128,2880]{0,1:T(8,128)(2,1)}), bf16[128,2880]{0,1:T(8,128)(2,1)}) %all-reduce.2.cloned.1.call-update) | async-done | bytes 737296 | tf_op jit(solution)/shard_map/psum | solution.py:71
  60.3 1.5 multiply_reduce_fusion
  61.8 2.3 convolution_bitcast_fusion
  64.2 87.9 %all_to_all.30 = bf16[16,1,40,2880]{3,2,1,0:T(8,128)(2,1)S(1)} all-to-all(bf16[16,1,40,2880]{3,2,1,0:T(8,128)(2,1)S(1)} %convolution_bitcast_fusion), channel_id=1, replica_groups=mesh['groups'=2,'ctx'=4,'head'=2,'sub'=2] {'ctx'}, dimensions={0} | all-to-all | bytes 7372800 | tf_op jit(solution)/shard_map/all_to_all | solution.py:88
  152.1 2.1 copy.65
  154.2 18.0 %fusion.47 = f32[4,160,1440]{2,1,0:T(8,128)} fusion(bf16[4,160,2880]{2,1,0:T(8,128)(2,1)} %bitcast.85, bf16[4,2880,1440]{1,2,0:T(8,128)(2,1)} %bitcast.86), kind=kOutput, calls=%fused_computation.82 | convolution fusion | flops 5308416000 | bytes 40550400 | tf_op jit(solution)/shard_map/erd,edf->erf/dot_general | solution.py:92
  172.2 12.4 %convolution_convert_fusion = bf16[4,160,2880]{2,1,0:T(8,128)(2,1)} fusion(bf16[4,2880,720]{1,2,0:T(8,128)(2,1)} %param.21, f32[4,160,1440]{2,1,0:T(8,128)} %fusion.47), kind=kOutput, calls=%fused_computation.2 | convolution fusion | flops 2659737600 | bytes 23961600 | tf_op jit(solution)/shard_map/ecf,erf->cer/dot_general | solution.py:105
  184.6 6.0 %copy.70 = bf16[2880,640]{1,0:T(8,128)(2,1)} copy(bf16[2880,640]{0,1:T(8,128)(2,1)} %bitcast.90) | data formatting | bytes 7372800
  190.7 39.9 %reduce-scatter.4.cloned.1.call-done = bf16[720,640]{1,0:T(8,128)(2,1)} async-done(((bf16[2880,640]{1,0:T(8,128)(2,1)}), bf16[720,640]{1,0:T(8,128)(2,1)}) %reduce-scatter.4.cloned.1.call-update) | async-done | bytes 921616
  230.6 1.6 copy.71
  232.2 1.0 copy.66
  233.2 4.6 %all-to-all-start.1 = ((bf16[720,4,4,40]{0,3,1,2:T(8,128)(2,1)}), bf16[720,4,4,40]{0,3,1,2:T(8,128)(2,1)S(1)}, u32[]{:S(2)}, u32[]{:S(2)}) async-start(bf16[720,4,4,40]{0,3,1,2:T(8,128)(2,1)} %copy.66), calls=%async_computation.1 | async-start | bytes 1966080 | tf_op jit(solution)/shard_map/all_to_all | solution.py:113
  237.8 0.1 select_reduce_fusion
  238.1 24.0 %all-to-all-done.1 = bf16[720,4,4,40]{0,3,1,2:T(8,128)(2,1)S(1)} async-done(((bf16[720,4,4,40]{0,3,1,2:T(8,128)(2,1)}), bf16[720,4,4,40]{0,3,1,2:T(8,128)(2,1)S(1)}, u32[]{:S(2)}, u32[]{:S(2)}) %all-to-all-start.1) | async-done | bytes 921632 | tf_op jit(solution)/shard_map/all_to_all | solution.py:113
  262.1 1.9 fusion.11
  (39 shorter events, 0.9 us)
Async XLA Ops:
  6.5 53.8 %all-reduce.2.cloned.1.call-start = ((), (), s32[]{:S(2)}) async-start(), calls=%async_computation.3 | async-start | bytes 1474560 | tf_op jit(solution)/shard_map/psum | solution.py:71
  7.6 8.7 %collective-permute-start = (bf16[128,4,128]{0,2,1:T(8,128)(2,1)S(1)}, bf16[128,4,128]{0,2,1:T(8,128)(2,1)S(1)}, u32[]{:S(2)}, u32[]{:S(2)}) collective-permute-start(bf16[128,4,128]{0,2,1:T(8,128)(2,1)S(1)} %copy.56), channel_id=1, source_target_pairs={{0,4},{4,8},{8,12},{1,5},{5,9},{9,13},{2,6},{6,10},{10,14},{3,7},{... | collective-permute-start | bytes 393224 | tf_op jit(solution)/shard_map/ppermute | solution.py:19
  16.3 1.3 copy-start.3
  17.0 0.7 copy-start.5
  19.3 4.5 %copy-start.1 = (bf16[128,720]{0,1:T(8,128)(2,1)S(1)}, bf16[128,720]{0,1:T(8,128)(2,1)}, u32[]{:S(2)}) copy-start(bf16[128,720]{0,1:T(8,128)(2,1)} %param.16) | copy-start | bytes 552964
  23.8 1.1 slice-start
  23.8 1.4 copy-start.4
  23.9 37.9 %copy-start.2 = (f32[2880]{0:T(1024)S(1)}, f32[2880]{0:T(1024)}, u32[]{:S(2)}) copy-start(f32[2880]{0:T(1024)} %param.17) | copy-start | bytes 34564
  24.9 205.7 %reduce-scatter.4.cloned.1.call-start = ((), (), s32[]{:S(2)}) async-start(), calls=%async_computation.4 | async-start | bytes 4608000
  232.2 5.7 %copy-start.6 = (f32[128,4]{0,1:T(4,128)S(1)}, f32[128,4]{0,1:T(4,128)}, u32[]{:S(2)}) copy-start(f32[128,4]{0,1:T(4,128)} %param.19) | copy-start | bytes 6148
  232.2 5.8 %copy-start = (bf16[128,2880]{0,1:T(8,128)(2,1)S(1)}, bf16[128,2880]{0,1:T(8,128)(2,1)}, u32[]{:S(2)}) copy-start(bf16[128,2880]{0,1:T(8,128)(2,1)} %all-reduce.2.cloned.1.call-done) | copy-start | bytes 2211844
  233.2 28.9 %all-to-all-start.1 = ((bf16[720,4,4,40]{0,3,1,2:T(8,128)(2,1)}), bf16[720,4,4,40]{0,3,1,2:T(8,128)(2,1)S(1)}, u32[]{:S(2)}, u32[]{:S(2)}) async-start(bf16[720,4,4,40]{0,3,1,2:T(8,128)(2,1)} %copy.66), calls=%async_computation.1 | async-start | bytes 1966080 | tf_op jit(solution)/shard_map/all_to_all | solution.py:113
Sparse Core Ops, SparseCore 0:
  25.0 35.2 all-reduce.1
  190.8 39.7 reduce-scatter.3
where the time goes:
time: 271 us
  waiting for transfers between devices  98.9 us (36%)
  blocking collectives  87.9 us (32%)
  matrix products  40.2 us (15%)
  local copies, waits for them, and re-layouts  15.5 us (6%)
  between operations  13.7 us (5%)
  starting transfers between devices  9.6 us (4%)
  other arithmetic  5.06 us (2%)
    all_to_all x1, blocking collectives, shards(): lax.all_to_all(outgoing, 'ctx', split_axis=0, concat_axis=1, tiled=True)  87.9 us
    unnamed x3, waiting for transfers between devices  40 us
    psum x1, waiting for transfers between devices, shards(): lax.psum(projected_attn.astype(jnp.bfloat16), ('head', 'sub'))  34.9 us
    all_to_all x1, waiting for transfers between devices, shards(): lax.all_to_all(regrouped.astype(jnp.bfloat16), 'ctx', split_axis=2, conca...  24 us
    dot_general x1, matrix products, shards(): jnp.einsum('erd,edf->erf', expert_rows, gate_up.reshape(local_experts, D,...  18 us
    dot_general x1, matrix products, shards(): jnp.einsum('ecf,erf->cer', down_weight, activated, preferred_element_type...  12.4 us
    unnamed x19, local copies, waits for them, and re-layouts  10.6 us
  transfers between devices with their start and end apart: 4, of which 3 were waited for; matrix products, arithmetic and copies ran while one was open for 2% of the time, Pallas kernels for 0%

commit v1 on v0

--- a/solution.py
+++ b/solution.py
@@ -1,6 +1,10 @@
+import functools
+
 import jax
 import jax.numpy as jnp
 from jax import lax
+from jax.experimental import pallas as pl
+from jax.experimental.pallas import tpu as pltpu
 from jax.sharding import PartitionSpec as P
 
 D = 2880
@@ -128,9 +132,418 @@
     return (resid_cols + mixture).astype(jnp.bfloat16)
 
 
+BF = jnp.bfloat16
+F32 = jnp.float32
+MESH = pl.DeviceIdType.MESH
+ROWS = 48
+EXTRA = 16
+NT = (((1,), (1,)), ((), ()))
+TN = (((0,), (0,)), ((), ()))
+
+
+def fused_kernel(
+    q_ref,
+    kv_ref,
+    sinks_ref,
+    ow_hbm,
+    resid_ref,
+    gain_ref,
+    info_ref,
+    gu_hbm,
+    dn_hbm,
+    out_ref,
+    kvprev,
+    ow,
+    gu,
+    dn,
+    att,
+    pa,
+    ra,
+    hidden,
+    info,
+    xb,
+    xsel,
+    actt,
+    outs,
+    ptc,
+    mix,
+    rsib,
+    xq,
+    rx,
+    zq,
+    rz,
+    w_sem,
+    kv_sem,
+    info_send,
+    info_recv,
+    a_send,
+    a_recv,
+    b_send,
+    b_recv,
+    c_send,
+    csib_recv,
+    cx_recv,
+    cz_recv,
+):
+    g, c, h, s = (lax.axis_index(n) for n in ("groups", "ctx", "head", "sub"))
+    n_ctx = 4
+    toks = q_ref.shape[0]
+    share = resid_ref.shape[0]
+    experts = gu_hbm.shape[0]
+    gu_slots, dn_slots = gu.shape[0], dn.shape[0]
+    quarter = lambda hh, ss: hh * 2 + ss
+    me_j, x_j = quarter(h, s), quarter(1 - h, s)
+    sib, xdev = (g, c, h, 1 - s), (g, c, 1 - h, s)
+    zdev = lambda cc: (g, cc, h, s)
+    rows_of = lambda j: pl.ds(pl.multiple_of(j * share, 16), share)
+
+    def remote(src, dst, send, recv, dev):
+        return pltpu.make_async_remote_copy(
+            src_ref=src, dst_ref=dst, send_sem=send, recv_sem=recv, device_id=dev, device_id_type=MESH
+        )
+
+    ow_copy = pltpu.make_async_copy(ow_hbm, ow, w_sem.at[0])
+    gu_copy = lambda e, slot: pltpu.make_async_copy(gu_hbm.at[e], gu.at[slot], w_sem.at[1 + slot])
+    dn_copy = lambda e, slot: pltpu.make_async_copy(
+        dn_hbm.at[e], dn.at[slot], w_sem.at[1 + gu_slots + slot]
+    )
+    ow_copy.start()
+    for e in range(gu_slots):
+        gu_copy(e, e).start()
+        if e < dn_slots:
+            dn_copy(e, e).start()
+
+    barrier = pltpu.get_barrier_semaphore()
+    others = [lax.rem(c + i, n_ctx) for i in range(1, n_ctx)]
+    for dev in [sib, xdev] + [zdev(o) for o in others]:
+        pl.semaphore_signal(barrier, inc=1, device_id=dev, device_id_type=MESH)
+    pl.semaphore_wait(barrier, 2 + len(others))
+
+    kv_out = remote(kv_ref, kvprev, kv_sem.at[0], kv_sem.at[1], zdev(lax.rem(c + 1, n_ctx)))
+
+    @pl.when(c < n_ctx - 1)
+    def _():
+        kv_out.start()
+
+    info[c] = info_ref[...]
+    for i, o in enumerate(others):
+        remote(info_ref, info.at[c], info_send.at[i], info_recv.at[c], zdev(o)).start()
+
+    @pl.when(c > 0)
+    def _():
+        kv_out.wait_recv()
+
+    @pl.when(c == 0)
+    def _():
+        kvprev[...] = jnp.zeros_like(kvprev)
+
+    t_pos = lax.broadcasted_iota(jnp.int32, (toks, 2 * toks), 0)
+    k_pos = lax.broadcasted_iota(jnp.int32, (toks, 2 * toks), 1)
+    first = jnp.where(c == 0, toks, 0)
+    allowed = (k_pos <= t_pos + WIN) & (k_pos > t_pos) & (k_pos >= first)
+    group = HEADS // KV_HEADS
+
+    def head_pair(p, carry):
+        kv_cols = pl.ds(pl.multiple_of((2 * p // group) * 2 * HD, 2 * HD), 2 * HD)
+        q_cols = pl.ds(pl.multiple_of(p * 2 * HD, 2 * HD), 2 * HD)
+        window = jnp.concatenate([kvprev[:, kv_cols], kv_ref[:, kv_cols]], 0)
+        keys, values = window[:, :HD], window[:, HD:]
+        pair = q_ref[:, q_cols]
+        done = []
+        for i in range(2):
+            sink = sinks_ref[2 * p + i]
+            scores = lax.dot_general(
+                pair[:, i * HD : (i + 1) * HD], keys, NT, preferred_element_type=F32
+            ) * HD ** (-0.5)
+            masked = jnp.where(allowed, scores, -1e30)
+            highest = jnp.maximum(jnp.max(masked, -1, keepdims=True), sink)
+            weights = jnp.where(allowed, jnp.exp(masked - highest), 0.0)
+            totals = jnp.sum(weights, -1, keepdims=True) + jnp.exp(sink - highest)
+            weighed = jnp.dot(weights.astype(BF), values, preferred_element_type=F32)
+            done.append(weighed / totals)
+        att[:, q_cols] = jnp.concatenate(done, 1).astype(BF)
+        return carry
+
+    lax.fori_loop(0, q_ref.shape[1] // (2 * HD), head_pair, 0)
+
+    ow_copy.wait()
+
+    def projected(j):
+        return lax.dot_general(ow[rows_of(j), :], att[...], NT, preferred_element_type=F32)
+
+    for i, hh in enumerate((1 - h, h)):
+        pa[i] = projected(quarter(hh, 1 - s)).astype(BF)
+        remote(pa.at[i], ra.at[i], a_send.at[i], a_recv.at[i], sib).start()
+    across = projected(x_j)
+    remote(pa.at[0], ra.at[0], a_send.at[0], a_recv.at[0], sib).wait_recv()
+    pa[2] = (across + ra[0].astype(F32)).astype(BF)
+    to_x = remote(pa.at[2], ra.at[2], a_send.at[2], a_recv.at[2], xdev)
+    to_x.start()
+    own = projected(me_j) + resid_ref[...].astype(F32)
+    remote(pa.at[1], ra.at[1], a_send.at[1], a_recv.at[1], sib).wait_recv()
+    own = own + ra[1].astype(F32)
+    to_x.wait_recv()
+    own = own + ra[2].astype(F32)
+    hidden[...] = own
+
+    xb[me_j * n_ctx + c, :share, :] = (own * gain_ref[...]).astype(BF)
+    squares = jnp.sum(own * own, 0, keepdims=True)
+    upper = squares.astype(BF).astype(F32)
+    line = lax.broadcasted_iota(jnp.int32, (EXTRA, toks), 0)
+    xb[me_j * n_ctx + c, share:, :] = jnp.where(
+        line == 0, upper, jnp.where(line == 1, squares - upper, 0.0)
+    ).astype(BF)
+
+    def block(j, cc, send, dev):
+        k = j * n_ctx + cc
+        return remote(xb.at[k], xb.at[k], b_send.at[send], b_recv.at[k], dev)
+
+    order = [c] + others
+    for i, o in enumerate(others):
+        block(me_j, c, i, zdev(o)).start()
+    for i, o in enumerate(order):
+        if i > 0:
+            block(me_j, o, 0, sib).wait_recv()
+        block(me_j, o, 3 + i, xdev).start()
+        block(me_j, o, 7 + i, sib).start()
+    for i, o in enumerate(order):
+        block(x_j, o, 0, sib).wait_recv()
+        block(x_j, o, 11 + i, sib).start()
+    for o in others:
+        remote(info_ref, info.at[o], info_send.at[0], info_recv.at[o], sib).wait_recv()
+    for o in order:
+        for hh in (h, 1 - h):
+            block(quarter(hh, 1 - s), o, 0, sib).wait_recv()
+
+    total_sq = jnp.zeros((n_ctx, toks), F32)
+    for j in range(4):
+        tails = [
+            jnp.sum(xb[j * n_ctx + cc, share:, :].astype(F32), 0, keepdims=True)
+            for cc in range(n_ctx)
+        ]
+        total_sq = total_sq + jnp.concatenate(tails, 0)
+    scale = lax.rsqrt(total_sq / D + 1e-05)
+    scale = jnp.concatenate([scale[cc : cc + 1] for cc in range(n_ctx)], 1)
+    s_hi = scale.astype(BF).astype(F32)
+    s_mid = (scale - s_hi).astype(BF).astype(F32)
+    s_lo = scale - s_hi - s_mid
+    tri = (
+        lax.broadcasted_iota(jnp.int32, (toks, toks), 0)
+        < lax.broadcasted_iota(jnp.int32, (toks, toks), 1)
+    )
+    tri = jnp.where(tri, 1.0, 0.0).astype(BF)
+    line8 = lax.broadcasted_iota(jnp.int32, (16, n_ctx * toks), 0)
+    scales = jnp.where(
+        line8 == 0, s_hi, jnp.where(line8 == 1, s_mid, jnp.where(line8 == 2, s_lo, 0.0))
+    ).astype(BF)
+    all_rows = lax.broadcasted_iota(jnp.int32, (n_ctx * ROWS, toks), 0).astype(F32)
+    slot_rows = lax.broadcasted_iota(jnp.int32, (ROWS, toks), 0).astype(F32)
+    tile = 240 if share % 240 == 0 else share
+    width = 768
+
+    def expert(e, carry):
+        name = (c * experts + e).astype(F32)
+        places, factors = [], []
+        for cc in range(n_ctx):
+            routing = info[cc]
+            same = jnp.where(routing[:TOP] == name, 1.0, 0.0)
+            named = jnp.sum(same, 0, keepdims=True)
+            factor = jnp.sum(same * routing[TOP:], 0, keepdims=True)
+            rank = jnp.dot(
+                jnp.broadcast_to(named, (16, toks)).astype(BF), tri, preferred_element_type=F32
+            )[:1]
+            place = jnp.where(named > 0, rank, -1.0)
+            ptc[cc, pl.ds(pl.multiple_of(e * ROWS, 16), ROWS), :] = jnp.where(
+                slot_rows == place, 1.0, 0.0
+            ).astype(BF)
+            places.append(jnp.where(all_rows == jnp.where(named > 0, rank + cc * ROWS, -1.0), 1.0, 0.0))
+            factors.append(jnp.sum(places[-1] * factor, 1, keepdims=True))
+        pick = jnp.concatenate(places, 1).astype(BF)
+        factor = factors[0] + factors[1] + factors[2] + factors[3]
+        row_scale = jnp.sum(
+            lax.dot_general(scales, pick, NT, preferred_element_type=F32), 0, keepdims=True
+        )
+
+        def select(j, carry):
+            features = jnp.concatenate([xb[j * n_ctx + cc, :share, :] for cc in range(n_ctx)], 1)
+            xsel[rows_of(j), :] = lax.dot_general(
+                features, pick, NT, preferred_element_type=F32
+            ).astype(BF)
+            return carry
+
+        lax.fori_loop(0, 4, select, 0)
+        slot = lax.rem(e, gu_slots)
+        gu_copy(e, slot).wait()
+
+        def up_gate(i, carry):
+            rows = pl.ds(pl.multiple_of(i * tile, 16), tile)
+            gate = jnp.dot(gu[slot, 0, rows, :], xsel[...], preferred_element_type=F32) * row_scale
+            up = jnp.dot(gu[slot, 1, rows, :], xsel[...], preferred_element_type=F32) * row_scale
+            actt[rows, :] = ((up + 1.0) * gate * jax.nn.sigmoid(1.702 * gate)).astype(BF)
+            return carry
+
+        lax.fori_loop(0, share // tile, up_gate, 0)
+
+        @pl.when(e + gu_slots < experts)
+        def _():
+            gu_copy(e + gu_slots, slot).start()
+
+        dslot = lax.rem(e, dn_slots)
+        dn_copy(e, dslot).wait()
+        act = actt[...]
+        for lo in range(0, D, width):
+            hi = min(D, lo + width)
+            res = lax.dot_general(act, dn[dslot, :, lo:hi], TN, preferred_element_type=F32)
+            res = (res * factor).astype(BF)
+            for cc in range(n_ctx):
+                outs[cc, pl.ds(pl.multiple_of(e * ROWS, 16), ROWS), lo:hi] = res[
+                    cc * ROWS : (cc + 1) * ROWS
+                ]
+
+        @pl.when(e + dn_slots < experts)
+        def _():
+            dn_copy(e + dn_slots, dslot).start()
+
+        return carry
+
+    lax.fori_loop(0, experts, expert, 0)
+
+    back = others + [c]
+    for i, o in enumerate(back):
+        for lo in range(0, D, width):
+            hi = min(D, lo + width)
+            mix[o, lo:hi, :] = lax.dot_general(
+                outs[o, :, lo:hi], ptc[o], TN, preferred_element_type=F32
+            ).astype(BF)
+        for hh in range(2):
+            remote(
+                mix.at[o, rows_of(quarter(hh, 1 - s))],
+                rsib.at[o * 2 + hh],
+                c_send.at[i * 2 + hh],
+                csib_recv.at[o * 2 + hh],
+                sib,
+            ).start()
+
+    def wait_sib(o, hh):
+        k = o * 2 + hh
+        remote(rsib.at[k], rsib.at[k], c_send.at[0], csib_recv.at[k], sib).wait_recv()
+        return rsib[k].astype(F32)
+
+    for i, o in enumerate(back):
+        xq[o] = (mix[o, rows_of(x_j), :].astype(F32) + wait_sib(o, 1 - h)).astype(BF)
+        remote(xq.at[o], rx.at[o], c_send.at[8 + i], cx_recv.at[o], xdev).start()
+    for i, o in enumerate(back):
+        part = mix[o, rows_of(me_j), :].astype(F32) + wait_sib(o, h)
+        remote(xq.at[o], rx.at[o], c_send.at[0], cx_recv.at[o], xdev).wait_recv()
+        part = part + rx[o].astype(F32)
+        if i < n_ctx - 1:
+            zq[i] = part.astype(BF)
+            remote(zq.at[i], rz.at[c], c_send.at[12 + i], cz_recv.at[c], zdev(o)).start()
+        else:
+            hidden[...] = hidden[...] + part
+    for o in others:
+        remote(zq.at[0], rz.at[o], c_send.at[0], cz_recv.at[o], sib).wait_recv()
+        hidden[...] = hidden[...] + rz[o].astype(F32)
+    out_ref[...] = hidden[...].astype(BF)
+
+    @pl.when(c < n_ctx - 1)
+    def _():
+        kv_out.wait_send()
+
+    for i in range(n_ctx - 1):
+        remote(info_ref, info.at[c], info_send.at[i], info_recv.at[c], sib).wait_send()
+    for i in range(3):
+        remote(pa.at[i], ra.at[i], a_send.at[i], a_recv.at[i], sib).wait_send()
+    for i in range(15):
+        block(me_j, c, i, sib).wait_send()
+    for i in range(15):
+        remote(rx.at[0], rx.at[0], c_send.at[i], cx_recv.at[0], sib).wait_send()
+
+
+def fused_shards(
+    queries,
+    keys_values,
+    sinks,
+    out_weight,
+    residual_in,
+    norm_gain,
+    expert_ids,
+    gate_weights,
+    gate_up,
+    down_weight,
+):
+    toks = queries.shape[0]
+    share = residual_in.shape[1]
+    experts = gate_up.shape[0]
+    kv_heads = sinks.shape[0] * KV_HEADS // HEADS
+    kv = lax.dynamic_slice_in_dim(keys_values, lax.axis_index("sub") * kv_heads, kv_heads, 1)
+    kv = kv.reshape(toks, kv_heads * 2 * HD)
+    gain = lax.dynamic_slice_in_dim(norm_gain, lax.axis_index(("head", "sub")) * share, share, 0)
+    info = jnp.concatenate([expert_ids.T.astype(F32), gate_weights.T], 0)
+    vmem = pl.BlockSpec(memory_space=pltpu.VMEM)
+    hbm = pl.BlockSpec(memory_space=pl.ANY)
+    gu_slots, dn_slots = min(3, experts), min(2, experts)
+    dma = pltpu.SemaphoreType.DMA
+    out = pl.pallas_call(
+        fused_kernel,
+        out_shape=jax.ShapeDtypeStruct((share, toks), BF),
+        in_specs=[vmem, vmem, pl.BlockSpec(memory_space=pltpu.SMEM), hbm, vmem, vmem, vmem, hbm, hbm],
+        out_specs=vmem,
+        scratch_shapes=[
+            pltpu.VMEM(kv.shape, BF),
+            pltpu.VMEM((D, out_weight.shape[0]), BF),
+            pltpu.VMEM((gu_slots, 2, share, D), BF),
+            pltpu.VMEM((dn_slots, share, D), BF),
+            pltpu.VMEM(queries.shape, BF),
+            pltpu.VMEM((3, share, toks), BF),
+            pltpu.VMEM((3, share, toks), BF),
+            pltpu.VMEM((share, toks), F32),
+            pltpu.VMEM((4, 2 * TOP, toks), F32),
+            pltpu.VMEM((16, share + EXTRA, toks), BF),
+            pltpu.VMEM((D, 4 * ROWS), BF),
+            pltpu.VMEM((share, 4 * ROWS), BF),
+            pltpu.VMEM((4, experts * ROWS, D), BF),
+            pltpu.VMEM((4, experts * ROWS, toks), BF),
+            pltpu.VMEM((4, D, toks), BF),
+            pltpu.VMEM((8, share, toks), BF),
+            pltpu.VMEM((4, share, toks), BF),
+            pltpu.VMEM((4, share, toks), BF),
+            pltpu.VMEM((3, share, toks), BF),
+            pltpu.VMEM((4, share, toks), BF),
+            dma((1 + gu_slots + dn_slots,)),
+            dma((2,)),
+            dma((3,)),
+            dma((4,)),
+            dma((3,)),
+            dma((3,)),
+            dma((15,)),
+            dma((16,)),
+            dma((15,)),
+            dma((8,)),
+            dma((4,)),
+            dma((4,)),
+        ],
+        compiler_params=pltpu.CompilerParams(
+            collective_id=0, has_side_effects=True, vmem_limit_bytes=63 * 1024 * 1024
+        ),
+    )(
+        queries,
+        kv,
+        sinks,
+        out_weight.T,
+        residual_in.T,
+        gain[:, None],
+        info,
+        gate_up.transpose(0, 2, 3, 1),
+        down_weight.transpose(0, 2, 1),
+    )
+    return out.T
+
+
 def solution(mesh):
+    fits = mesh.shape["ctx"] == 4 and mesh.shape["head"] == 2 and mesh.shape["sub"] == 2
     return jax.shard_map(
-        shards,
+        fused_shards if fits else shards,
         mesh=mesh,
         in_specs=(
             P(("groups", "ctx"), ("head", "sub")),

time: 271 us -> 113 us (0.42)
  Pallas kernels: 0 us -> 106 us
  waiting for transfers between devices: 98.9 us -> 0 us
  blocking collectives: 87.9 us -> 0 us
  matrix products: 40.2 us -> 0 us
  between operations: 13.7 us -> 0.02 us
  local copies, waits for them, and re-layouts: 15.5 us -> 4.22 us
  starting transfers between devices: 9.6 us -> 0 us
  other arithmetic: 5.06 us -> 2 us
    pallas_call x0 -> x1, Pallas kernels: none -> 106 us  [fused_shards(): pl.pallas_call(fused_kernel, out_shape=jax.ShapeDtypeStruct((share, toks)...]
    all_to_all x1 -> x0, blocking collectives: 87.9 us -> none  [shards(): lax.all_to_all(outgoing, 'ctx', split_axis=0, concat_axis=1, tiled=True)]
    dot_general x7 -> x0, matrix products: 40.2 us -> none  [the longest x1 18 us: shards(): jnp.einsum('erd,edf->erf', expert_rows, gate_up.reshape(local_experts, D,...]
    unnamed x3 -> x0, waiting for transfers between devices: 40 us -> none
    psum x1 -> x0, waiting for transfers between devices: 34.9 us -> none  [shards(): lax.psum(projected_attn.astype(jnp.bfloat16), ('head', 'sub'))]
    all_to_all x1 -> x0, waiting for transfers between devices: 24 us -> none  [shards(): lax.all_to_all(regrouped.astype(jnp.bfloat16), 'ctx', split_axis=2, conca...]
    unnamed x19 -> x4, local copies, waits for them, and re-layouts: 10.6 us -> 1.73 us
    ppermute x1 -> x0, starting transfers between devices: 4.94 us -> none  [from_behind(): lax.ppermute(value, axis, [(source, source + steps) for source in range(l...]
  transfers between devices with their start and end apart: 4 -> 0, of which waited for: 3 -> 0; matrix products, arithmetic and copies ran while one was open for 2% -> 0% of each run, Pallas kernels for 0% -> 0%
where the time goes in v1:
time: 113 us; the launch traced here: 112 us
  Pallas kernels  106 us (94%)
  local copies, waits for them, and re-layouts  4.22 us (4%)
  other arithmetic  2 us (2%)
    pallas_call x1, Pallas kernels, fused_shards(): pl.pallas_call(fused_kernel, out_shape=jax.ShapeDtypeStruct((share, toks)...  106 us

profile of v1, /device:TPU:0, one launch (start us, length us, event | category | flops | bytes accessed | tf_op | source)
XLA Modules:
  0.0 112.4 jit_solution(1223630591295918999)
XLA Ops:
  0.0 0.0 copy-start
  0.0 0.7 convert_bitcast_fusion
  0.7 1.3 %pad_maximum_fusion.info_ref = f32[8,128]{1,0:T(8,128)} fusion(f32[4,128]{1,0:T(4,128)} %bitcast.15, f32[4,128]{1,0:T(4,128)S(1)} %convert_bitcast_fusion), kind=kLoop, calls=%fused_computation | loop fusion | flops 1024 | bytes 8192 | tf_op jit(solution)/shard_map/concatenate | solution.py:482
  2.0 0.8 dynamic_slice.7
  2.8 0.0 copy-done
  2.8 0.1 constant_dynamic-slice_fusion
  2.9 0.1 copy.14
  3.0 0.7 copy.12.kv_ref
  3.7 0.9 broadcast_in_dim.4.gain_ref
  4.6 106.1 %shard_map.100 = bf16[720,128]{1,0:T(8,128)(2,1)} custom-call(bf16[128,1024]{1,0:T(8,128)(2,1)} %q_ref.1, bf16[128,256]{1,0:T(8,128)(2,1)} %copy.12.kv_ref, f32[16]{0:T(128)} %sinks_ref.1, bf16[2880,1024]{1,0:T(8,128)(2,1)} %bitcast.11, bf16[720,128]{1,0:T(8,128)(2,1)} %bitcast.14, f32[720,1]{1,0:T(8,128)} %broadcast_in_dim.4.gain_ref, ...), custom_call_target="tpu_custom_call" | custom-call | tf_op jit(solution)/shard_map/pallas_call | solution.py:487
  110.8 1.6 %copy.16 = bf16[128,720]{0,1:T(8,128)(2,1)} copy(bf16[128,720]{0,1:T(8,128)(2,1)} %bitcast.12) | data formatting | bytes 368640
Async XLA Ops:
  0.0 2.8 %copy-start = (bf16[128,4,128]{2,1,0:T(4,128)(2,1)S(1)}, bf16[128,4,128]{2,1,0:T(4,128)(2,1)}, u32[]{:S(2)}) copy-start(bf16[128,4,128]{2,1,0:T(4,128)(2,1)} %param.11) | copy-start | bytes 393220

commit v2 on v1

--- a/solution.py
+++ b/solution.py
@@ -148,10 +148,14 @@
     ow_hbm,
     resid_ref,
     gain_ref,
-    info_ref,
+    ids_ref,
+    gates_ref,
     gu_hbm,
     dn_hbm,
     out_ref,
+    kvown,
+    picks,
+    factors_of,
     kvprev,
     ow,
     gu,
@@ -168,9 +172,7 @@
     ptc,
     mix,
     rsib,
-    xq,
     rx,
-    zq,
     rz,
     w_sem,
     kv_sem,
@@ -213,21 +215,32 @@
         if e < dn_slots:
             dn_copy(e, e).start()
 
+    heads = kvown.shape[1] // (2 * HD)
+    for p in range(heads):
+        kvown[:, p * 2 * HD : (p + 1) * 2 * HD] = jnp.where(
+            s == 0, kv_ref[:, p, :], kv_ref[:, p + kv_ref.shape[1] - heads, :]
+        )
+    info[c, :TOP, :] = ids_ref[...].astype(F32)
+    info[c, TOP:, :] = gates_ref[...]
+
     barrier = pltpu.get_barrier_semaphore()
     others = [lax.rem(c + i, n_ctx) for i in range(1, n_ctx)]
     for dev in [sib, xdev] + [zdev(o) for o in others]:
         pl.semaphore_signal(barrier, inc=1, device_id=dev, device_id_type=MESH)
     pl.semaphore_wait(barrier, 2 + len(others))
 
-    kv_out = remote(kv_ref, kvprev, kv_sem.at[0], kv_sem.at[1], zdev(lax.rem(c + 1, n_ctx)))
+    kv_out = remote(kvown, kvprev, kv_sem.at[0], kv_sem.at[1], zdev(lax.rem(c + 1, n_ctx)))
 
     @pl.when(c < n_ctx - 1)
     def _():
         kv_out.start()
 
-    info[c] = info_ref[...]
     for i, o in enumerate(others):
-        remote(info_ref, info.at[c], info_send.at[i], info_recv.at[c], zdev(o)).start()
+        remote(info.at[c], info.at[c], info_send.at[i], info_recv.at[c], zdev(o)).start()
+
+    line4 = lax.broadcasted_iota(jnp.int32, gain_ref.shape, 0)
+    own_gain = jnp.sum(jnp.where(line4 == me_j, gain_ref[...], 0.0), 0, keepdims=True)
+    hidden[...] = jnp.broadcast_to(own_gain, (toks, share)).T
 
     @pl.when(c > 0)
     def _():
@@ -246,7 +259,7 @@
     def head_pair(p, carry):
         kv_cols = pl.ds(pl.multiple_of((2 * p // group) * 2 * HD, 2 * HD), 2 * HD)
         q_cols = pl.ds(pl.multiple_of(p * 2 * HD, 2 * HD), 2 * HD)
-        window = jnp.concatenate([kvprev[:, kv_cols], kv_ref[:, kv_cols]], 0)
+        window = jnp.concatenate([kvprev[:, kv_cols], kvown[:, kv_cols]], 0)
         keys, values = window[:, :HD], window[:, HD:]
         pair = q_ref[:, q_cols]
         done = []
@@ -264,7 +277,7 @@
         att[:, q_cols] = jnp.concatenate(done, 1).astype(BF)
         return carry
 
-    lax.fori_loop(0, q_ref.shape[1] // (2 * HD), head_pair, 0)
+    lax.fori_loop(0, q_ref.shape[1] // (2 * HD), head_pair, 0, unroll=2)
 
     ow_copy.wait()
 
@@ -284,9 +297,9 @@
     own = own + ra[1].astype(F32)
     to_x.wait_recv()
     own = own + ra[2].astype(F32)
+
+    xb[me_j * n_ctx + c, :share, :] = (own * hidden[...]).astype(BF)
     hidden[...] = own
-
-    xb[me_j * n_ctx + c, :share, :] = (own * gain_ref[...]).astype(BF)
     squares = jnp.sum(own * own, 0, keepdims=True)
     upper = squares.astype(BF).astype(F32)
     line = lax.broadcasted_iota(jnp.int32, (EXTRA, toks), 0)
@@ -298,50 +311,51 @@
         k = j * n_ctx + cc
         return remote(xb.at[k], xb.at[k], b_send.at[send], b_recv.at[k], dev)
 
-    order = [c] + others
-    for i, o in enumerate(others):
-        block(me_j, c, i, zdev(o)).start()
-    for i, o in enumerate(order):
-        if i > 0:
-            block(me_j, o, 0, sib).wait_recv()
-        block(me_j, o, 3 + i, xdev).start()
-        block(me_j, o, 7 + i, sib).start()
-    for i, o in enumerate(order):
-        block(x_j, o, 0, sib).wait_recv()
-        block(x_j, o, 11 + i, sib).start()
+    def both_ways(d, act):
+        for sign in (1,) if d == 0 else (-1, 1):
+            o = c + sign * d
+            inside = None if d == 0 else (o >= 0) & (o < n_ctx)
+
+            def at(o=o, sign=sign):
+                act(o, sign)
+
+            at() if inside is None else pl.when(inside)(at)
+
+    def z_step(d):
+        def act(o, sign):
+            if d > 0:
+                block(me_j, o, 0, sib).wait_recv()
+            for way in (1, -1) if d == 0 else (-sign,):
+
+                @pl.when((c + way >= 0) & (c + way < n_ctx))
+                def _():
+                    block(me_j, o, d if way > 0 else 3 + d, zdev(c + way)).start()
+
+            block(me_j, o, 6 + o, xdev).start()
+            block(me_j, o, 10 + o, sib).start()
+
+        both_ways(d, act)
+
+    def x_step(d):
+        def act(o, sign):
+            block(x_j, o, 0, sib).wait_recv()
+            block(x_j, o, 14 + o, sib).start()
+
+        both_ways(d, act)
+
+    z_step(0)
     for o in others:
-        remote(info_ref, info.at[o], info_send.at[0], info_recv.at[o], sib).wait_recv()
-    for o in order:
-        for hh in (h, 1 - h):
-            block(quarter(hh, 1 - s), o, 0, sib).wait_recv()
-
-    total_sq = jnp.zeros((n_ctx, toks), F32)
-    for j in range(4):
-        tails = [
-            jnp.sum(xb[j * n_ctx + cc, share:, :].astype(F32), 0, keepdims=True)
-            for cc in range(n_ctx)
-        ]
-        total_sq = total_sq + jnp.concatenate(tails, 0)
-    scale = lax.rsqrt(total_sq / D + 1e-05)
-    scale = jnp.concatenate([scale[cc : cc + 1] for cc in range(n_ctx)], 1)
-    s_hi = scale.astype(BF).astype(F32)
-    s_mid = (scale - s_hi).astype(BF).astype(F32)
-    s_lo = scale - s_hi - s_mid
+        remote(info.at[o], info.at[o], info_send.at[0], info_recv.at[o], sib).wait_recv()
+
     tri = (
         lax.broadcasted_iota(jnp.int32, (toks, toks), 0)
         < lax.broadcasted_iota(jnp.int32, (toks, toks), 1)
     )
     tri = jnp.where(tri, 1.0, 0.0).astype(BF)
-    line8 = lax.broadcasted_iota(jnp.int32, (16, n_ctx * toks), 0)
-    scales = jnp.where(
-        line8 == 0, s_hi, jnp.where(line8 == 1, s_mid, jnp.where(line8 == 2, s_lo, 0.0))
-    ).astype(BF)
     all_rows = lax.broadcasted_iota(jnp.int32, (n_ctx * ROWS, toks), 0).astype(F32)
     slot_rows = lax.broadcasted_iota(jnp.int32, (ROWS, toks), 0).astype(F32)
-    tile = 240 if share % 240 == 0 else share
-    width = 768
-
-    def expert(e, carry):
+
+    def route(e, carry):
         name = (c * experts + e).astype(F32)
         places, factors = [], []
         for cc in range(n_ctx):
@@ -358,27 +372,72 @@
             ).astype(BF)
             places.append(jnp.where(all_rows == jnp.where(named > 0, rank + cc * ROWS, -1.0), 1.0, 0.0))
             factors.append(jnp.sum(places[-1] * factor, 1, keepdims=True))
-        pick = jnp.concatenate(places, 1).astype(BF)
-        factor = factors[0] + factors[1] + factors[2] + factors[3]
-        row_scale = jnp.sum(
-            lax.dot_general(scales, pick, NT, preferred_element_type=F32), 0, keepdims=True
-        )
-
-        def select(j, carry):
-            features = jnp.concatenate([xb[j * n_ctx + cc, :share, :] for cc in range(n_ctx)], 1)
-            xsel[rows_of(j), :] = lax.dot_general(
-                features, pick, NT, preferred_element_type=F32
+        picks[e] = jnp.concatenate(places, 1).astype(BF)
+        factors_of[e] = factors[0] + factors[1] + factors[2] + factors[3]
+        return carry
+
+    lax.fori_loop(0, experts, route, 0)
+    z_step(1)
+    x_step(0)
+    z_step(2)
+    x_step(1)
+    z_step(3)
+    x_step(2)
+
+    def select(j):
+        features = jnp.concatenate([xb[j * n_ctx + cc, :share, :] for cc in range(n_ctx)], 1)
+
+        def one(e, carry):
+            xsel[e, rows_of(j), :] = lax.dot_general(
+                features, picks[e], NT, preferred_element_type=F32
             ).astype(BF)
             return carry
 
-        lax.fori_loop(0, 4, select, 0)
+        lax.fori_loop(0, experts, one, 0)
+
+    select(me_j)
+    order = [c] + others
+    for o in order:
+        block(quarter(h, 1 - s), o, 0, sib).wait_recv()
+    select(quarter(h, 1 - s))
+    x_step(3)
+    select(x_j)
+    for o in order:
+        block(quarter(1 - h, 1 - s), o, 0, sib).wait_recv()
+    select(quarter(1 - h, 1 - s))
+
+    total_sq = jnp.zeros((n_ctx, toks), F32)
+    for j in range(4):
+        tails = [
+            jnp.sum(xb[j * n_ctx + cc, share:, :].astype(F32), 0, keepdims=True)
+            for cc in range(n_ctx)
+        ]
+        total_sq = total_sq + jnp.concatenate(tails, 0)
+    scale = lax.rsqrt(total_sq / D + 1e-05)
+    scale = jnp.concatenate([scale[cc : cc + 1] for cc in range(n_ctx)], 1)
+    s_hi = scale.astype(BF).astype(F32)
+    s_mid = (scale - s_hi).astype(BF).astype(F32)
+    s_lo = scale - s_hi - s_mid
+    line8 = lax.broadcasted_iota(jnp.int32, (16, n_ctx * toks), 0)
+    scales = jnp.where(
+        line8 == 0, s_hi, jnp.where(line8 == 1, s_mid, jnp.where(line8 == 2, s_lo, 0.0))
+    ).astype(BF)
+    tile = 240 if share % 240 == 0 else share
+    width = 768
+
+    def expert(e, carry):
+        factor = factors_of[e]
+        row_scale = jnp.sum(
+            lax.dot_general(scales, picks[e], NT, preferred_element_type=F32), 0, keepdims=True
+        )
+
         slot = lax.rem(e, gu_slots)
         gu_copy(e, slot).wait()
 
         def up_gate(i, carry):
             rows = pl.ds(pl.multiple_of(i * tile, 16), tile)
-            gate = jnp.dot(gu[slot, 0, rows, :], xsel[...], preferred_element_type=F32) * row_scale
-            up = jnp.dot(gu[slot, 1, rows, :], xsel[...], preferred_element_type=F32) * row_scale
+            gate = jnp.dot(gu[slot, 0, rows, :], xsel[e], preferred_element_type=F32) * row_scale
+            up = jnp.dot(gu[slot, 1, rows, :], xsel[e], preferred_element_type=F32) * row_scale
             actt[rows, :] = ((up + 1.0) * gate * jax.nn.sigmoid(1.702 * gate)).astype(BF)
             return carry
 
@@ -430,19 +489,21 @@
         return rsib[k].astype(F32)
 
     for i, o in enumerate(back):
-        xq[o] = (mix[o, rows_of(x_j), :].astype(F32) + wait_sib(o, 1 - h)).astype(BF)
-        remote(xq.at[o], rx.at[o], c_send.at[8 + i], cx_recv.at[o], xdev).start()
+        mix[o, rows_of(x_j), :] = (
+            mix[o, rows_of(x_j), :].astype(F32) + wait_sib(o, 1 - h)
+        ).astype(BF)
+        remote(mix.at[o, rows_of(x_j)], rx.at[o], c_send.at[8 + i], cx_recv.at[o], xdev).start()
     for i, o in enumerate(back):
         part = mix[o, rows_of(me_j), :].astype(F32) + wait_sib(o, h)
-        remote(xq.at[o], rx.at[o], c_send.at[0], cx_recv.at[o], xdev).wait_recv()
+        remote(rx.at[o], rx.at[o], c_send.at[0], cx_recv.at[o], xdev).wait_recv()
         part = part + rx[o].astype(F32)
         if i < n_ctx - 1:
-            zq[i] = part.astype(BF)
-            remote(zq.at[i], rz.at[c], c_send.at[12 + i], cz_recv.at[c], zdev(o)).start()
+            mix[o, rows_of(me_j), :] = part.astype(BF)
+            remote(mix.at[o, rows_of(me_j)], rz.at[c], c_send.at[12 + i], cz_recv.at[c], zdev(o)).start()
         else:
             hidden[...] = hidden[...] + part
     for o in others:
-        remote(zq.at[0], rz.at[o], c_send.at[0], cz_recv.at[o], sib).wait_recv()
+        remote(rz.at[o], rz.at[o], c_send.at[0], cz_recv.at[o], sib).wait_recv()
         hidden[...] = hidden[...] + rz[o].astype(F32)
     out_ref[...] = hidden[...].astype(BF)
 
@@ -451,10 +512,17 @@
         kv_out.wait_send()
 
     for i in range(n_ctx - 1):
-        remote(info_ref, info.at[c], info_send.at[i], info_recv.at[c], sib).wait_send()
+        remote(info.at[c], info.at[c], info_send.at[i], info_recv.at[c], sib).wait_send()
     for i in range(3):
         remote(pa.at[i], ra.at[i], a_send.at[i], a_recv.at[i], sib).wait_send()
-    for i in range(15):
+    for d in range(3):
+        for way, first_o in ((1, c - d), (-1, c + d)):
+
+            @pl.when((c + way >= 0) & (c + way < n_ctx) & (first_o >= 0) & (first_o < n_ctx))
+            def _():
+                block(me_j, c, d if way > 0 else 3 + d, sib).wait_send()
+
+    for i in range(6, 18):
         block(me_j, c, i, sib).wait_send()
     for i in range(15):
         remote(rx.at[0], rx.at[0], c_send.at[i], cx_recv.at[0], sib).wait_send()
@@ -476,10 +544,6 @@
     share = residual_in.shape[1]
     experts = gate_up.shape[0]
     kv_heads = sinks.shape[0] * KV_HEADS // HEADS
-    kv = lax.dynamic_slice_in_dim(keys_values, lax.axis_index("sub") * kv_heads, kv_heads, 1)
-    kv = kv.reshape(toks, kv_heads * 2 * HD)
-    gain = lax.dynamic_slice_in_dim(norm_gain, lax.axis_index(("head", "sub")) * share, share, 0)
-    info = jnp.concatenate([expert_ids.T.astype(F32), gate_weights.T], 0)
     vmem = pl.BlockSpec(memory_space=pltpu.VMEM)
     hbm = pl.BlockSpec(memory_space=pl.ANY)
     gu_slots, dn_slots = min(3, experts), min(2, experts)
@@ -487,10 +551,13 @@
     out = pl.pallas_call(
         fused_kernel,
         out_shape=jax.ShapeDtypeStruct((share, toks), BF),
-        in_specs=[vmem, vmem, pl.BlockSpec(memory_space=pltpu.SMEM), hbm, vmem, vmem, vmem, hbm, hbm],
+        in_specs=[vmem, vmem, pl.BlockSpec(memory_space=pltpu.SMEM), hbm, vmem, vmem, vmem, vmem, hbm, hbm],
         out_specs=vmem,
         scratch_shapes=[
-            pltpu.VMEM(kv.shape, BF),
+            pltpu.VMEM((toks, kv_heads * 2 * HD), BF),
+            pltpu.VMEM((experts, 4 * ROWS, 4 * toks), BF),
+            pltpu.VMEM((experts, 4 * ROWS, 1), F32),
+            pltpu.VMEM((toks, kv_heads * 2 * HD), BF),
             pltpu.VMEM((D, out_weight.shape[0]), BF),
             pltpu.VMEM((gu_slots, 2, share, D), BF),
             pltpu.VMEM((dn_slots, share, D), BF),
@@ -500,7 +567,7 @@
             pltpu.VMEM((share, toks), F32),
             pltpu.VMEM((4, 2 * TOP, toks), F32),
             pltpu.VMEM((16, share + EXTRA, toks), BF),
-            pltpu.VMEM((D, 4 * ROWS), BF),
+            pltpu.VMEM((experts, D, 4 * ROWS), BF),
             pltpu.VMEM((share, 4 * ROWS), BF),
             pltpu.VMEM((4, experts * ROWS, D), BF),
             pltpu.VMEM((4, experts * ROWS, toks), BF),
@@ -508,15 +575,13 @@
             pltpu.VMEM((8, share, toks), BF),
             pltpu.VMEM((4, share, toks), BF),
             pltpu.VMEM((4, share, toks), BF),
-            pltpu.VMEM((3, share, toks), BF),
-            pltpu.VMEM((4, share, toks), BF),
             dma((1 + gu_slots + dn_slots,)),
             dma((2,)),
             dma((3,)),
             dma((4,)),
             dma((3,)),
             dma((3,)),
-            dma((15,)),
+            dma((18,)),
             dma((16,)),
             dma((15,)),
             dma((8,)),
@@ -528,12 +593,13 @@
         ),
     )(
         queries,
-        kv,
+        keys_values,
         sinks,
         out_weight.T,
         residual_in.T,
-        gain[:, None],
-        info,
+        norm_gain.reshape(-1, share),
+        expert_ids.T,
+        gate_weights.T,
         gate_up.transpose(0, 2, 3, 1),
         down_weight.transpose(0, 2, 1),
     )

time: 113 us -> 92.4 us (0.82)
  Pallas kernels: 106 us -> 89.2 us
  other arithmetic: 2 us -> 0 us
  local copies, waits for them, and re-layouts: 4.22 us -> 2.99 us
    pallas_call x1, Pallas kernels: 106 us -> 89.2 us  [fused_shards(): pl.pallas_call(fused_kernel, out_shape=jax.ShapeDtypeStruct((share, toks)...]
    concatenate x1 -> x0, other arithmetic: 1.28 us -> none  [fused_shards(): info = jnp.concatenate([expert_ids.T.astype(F32), gate_weights.T], 0)]
where the time goes in v2:
time: 92.4 us; the launch traced here: 92.2 us
  Pallas kernels  89.2 us (97%)
  local copies, waits for them, and re-layouts  2.99 us (3%)
    pallas_call x1, Pallas kernels, fused_shards(): pl.pallas_call(fused_kernel, out_shape=jax.ShapeDtypeStruct((share, toks)...  89.2 us

profile of v2, /device:TPU:0, one launch (start us, length us, event | category | flops | bytes accessed | tf_op | source)
XLA Modules:
  0.0 92.2 jit_solution(9585149668056264180)
XLA Ops:
  0.0 1.4 %reshape.3.gain_ref = f32[4,720]{1,0:T(4,128)} reshape(f32[2880]{0:T(1024)} %param.15) | data formatting | bytes 23040 | tf_op jit(solution)/shard_map/reshape | solution.py:600
  1.4 89.2 %shard_map.100 = bf16[720,128]{1,0:T(8,128)(2,1)} custom-call(bf16[128,1024]{1,0:T(8,128)(2,1)} %q_ref.1, bf16[128,4,128]{2,1,0:T(4,128)(2,1)} %kv_ref.1, f32[16]{0:T(128)} %sinks_ref.1, bf16[2880,1024]{1,0:T(8,128)(2,1)} %bitcast.9, bf16[720,128]{1,0:T(8,128)(2,1)} %bitcast.11, f32[4,720]{1,0:T(4,128)} %reshape.3.gain_ref, s32[4,128]{1,0:T(4,128)} %bitcast.12, ...), custom_call_target="tpu_custom_call" | custom-call | tf_op jit(solution)/shard_map/pallas_call | solution.py:551
  90.5 1.6 %copy.12 = bf16[128,720]{0,1:T(8,128)(2,1)} copy(bf16[128,720]{0,1:T(8,128)(2,1)} %bitcast.10) | data formatting | bytes 368640
